TPU v7x, 128 devices: a whole 4x4x4 slice. The times are simulated.
128 devices in a mesh: grp: 8 (over x, core), dev: 16 (over y, z).
Axes of the slice: x: 4, y: 4, z: 4, core: 2. Of those that a mesh axis runs over, the one named last changes fastest.
Arguments:
- emission: float32 [64, 524288], P(None, ('grp', 'dev')), may hold values from 0.2 to 2
- positions: float32 [3, 524288], P(None, ('grp', 'dev')), may hold values from -5 to 5
- normals: float32 [3, 524288], P(None, ('grp', 'dev')), may hold values from -3 to 3
- areas: float32 [524288], P(('grp', 'dev')), may hold values from 0.5 to 4
- material: int32 [524288], P(('grp', 'dev')), may hold values from 0 to 15
- reflect: float32 [64, 16], replicated, may hold values from 0.2 to 0.8
- pair_local: int32 [16384], P(('grp', 'dev')), may hold values from 0 to 31
- pair_device: int32 [16384, 1], P(('grp', 'dev')), may hold values from 0 to 127; in each aligned block of 128 rows (0 to 127, 128 to 255, ...) at most 2 rows name the same one
- pair_block: int32 [16384], P(('grp', 'dev')), may hold values from 0 to 31
Outputs:
- radiosity: float32 [64, 524288], P(None, ('grp', 'dev'))
Inputs may be any that keep to these rules, and one draw needn't show every extreme that they name: `pair_device`: among the 128 pairs of one device, at most 2 name the same device; some device's pairs name one device exactly 2 times.
All inputs are finite; a program needn't handle non-finite values.
Results may differ from a plain program's by a relative error of at most 0.00055.
Values may be sent and summed in bfloat16 or wider, within the bound.
A program may use at most 128 MiB of HBM per device.

v0:
```python
import math

import jax
import jax.numpy as jnp
from jax import lax
from jax.experimental import pallas as pl
from jax.experimental.pallas import tpu as pltpu
from jax.sharding import PartitionSpec as P

BLK = 128
SWEEPS = 2
AXES = ("grp", "dev")
GROUP = 8
softening = 0.5


def pack_kernel(index_ref, current_ref, areas_ref, out_ref, scaled_ref):
    blocks = scaled_ref.shape[0]

    @pl.when(pl.program_id(0) == 0)
    def _():
        for block in range(blocks):
            lanes = pl.ds(block * BLK, BLK)
            scaled_ref[block] = (current_ref[:, lanes] * areas_ref[:, lanes]).astype(jnp.bfloat16)

    base = pl.program_id(0) * out_ref.shape[0]
    for slot in range(out_ref.shape[0]):
        out_ref[slot] = scaled_ref[index_ref[base + slot]]


def pack(index, current, areas):
    slots = index.shape[0]
    bands, patches = current.shape
    step = min(slots, 32)
    return pl.pallas_call(
        pack_kernel,
        grid_spec=pltpu.PrefetchScalarGridSpec(
            num_scalar_prefetch=1,
            grid=(slots // step,),
            in_specs=[
                pl.BlockSpec((bands, patches), lambda i, index: (0, 0)),
                pl.BlockSpec((1, patches), lambda i, index: (0, 0)),
            ],
            out_specs=pl.BlockSpec((step, bands, BLK), lambda i, index: (i, 0, 0)),
            scratch_shapes=[pltpu.VMEM((patches // BLK, bands, BLK), jnp.bfloat16)],
        ),
        out_shape=jax.ShapeDtypeStruct((slots, bands, BLK), jnp.bfloat16),
        compiler_params=pltpu.CompilerParams(vmem_limit_bytes=32 << 20),
        cost_estimate=pl.CostEstimate(
            flops=0, bytes_accessed=slots * bands * BLK * 4, transcendentals=0
        ),
        name="pack",
    )(index, current, areas)


def tiles_kernel(mine_ref, other_ref, own_geometry_ref, geometry_ref, out_ref):
    base = pl.program_id(0) * out_ref.shape[0]
    for slot in range(out_ref.shape[0]):
        mine = mine_ref[base + slot]
        other = other_ref[base + slot]

        @pl.when(mine >= 0)
        def _():
            far = geometry_ref[other]
            far = jnp.concatenate([far, jnp.zeros((2, BLK), jnp.float32)], 0).T
            near = own_geometry_ref[mine]
            distance_sq = softening
            facing_near = 0.0
            facing_far = 0.0
            for axis_index in range(3):
                offset = far[:, axis_index : axis_index + 1] - near[axis_index : axis_index + 1]
                distance_sq = distance_sq + offset * offset
                facing_near = facing_near + near[3 + axis_index : 4 + axis_index] * offset
                facing_far = facing_far - far[:, 3 + axis_index : 4 + axis_index] * offset
            out_ref[slot] = (
                jnp.maximum(facing_near, 0.0)
                * jnp.maximum(facing_far, 0.0)
                / (math.pi * distance_sq * distance_sq)
            ).astype(jnp.bfloat16)


def tiles(mine, other, own_geometry, geometry):
    slots = mine.shape[0]
    step = GROUP
    return pl.pallas_call(
        tiles_kernel,
        grid_spec=pltpu.PrefetchScalarGridSpec(
            num_scalar_prefetch=2,
            grid=(slots // step,),
            in_specs=[
                pl.BlockSpec(own_geometry.shape, lambda i, mine, other: (0, 0, 0)),
                pl.BlockSpec(
                    geometry.shape, lambda i, mine, other: (0, 0, 0), pipeline_mode=pl.Buffered(1)
                ),
            ],
            out_specs=pl.BlockSpec((step, BLK, BLK), lambda i, mine, other: (i, 0, 0)),
        ),
        out_shape=jax.ShapeDtypeStruct((slots, BLK, BLK), jnp.bfloat16),
        compiler_params=pltpu.CompilerParams(vmem_limit_bytes=40 << 20),
        cost_estimate=pl.CostEstimate(
            flops=slots * BLK * BLK * 30, bytes_accessed=slots * BLK * BLK * 2, transcendentals=0
        ),
        name="tiles",
    )(mine, other, own_geometry, geometry)


def apply_kernel(mine_ref, values_ref, tiles_ref, start_ref, out_ref):
    @pl.when(pl.program_id(0) == 0)
    def _():
        out_ref[...] = start_ref[...]

    base = pl.program_id(0) * values_ref.shape[0]
    for slot in range(values_ref.shape[0]):
        mine = mine_ref[base + slot]

        @pl.when(mine >= 0)
        def _():
            lanes = pl.ds(pl.multiple_of(mine * BLK, BLK), BLK)
            out_ref[:, lanes] += jnp.dot(
                values_ref[slot], tiles_ref[slot], preferred_element_type=jnp.float32
            )


def apply(mine, values, kernel_tiles, start):
    slots, bands, _ = values.shape
    step = GROUP
    whole = pl.BlockSpec(start.shape, lambda i, mine: (0, 0))
    return pl.pallas_call(
        apply_kernel,
        grid_spec=pltpu.PrefetchScalarGridSpec(
            num_scalar_prefetch=1,
            grid=(slots // step,),
            in_specs=[
                pl.BlockSpec((step, bands, BLK), lambda i, mine: (i, 0, 0)),
                pl.BlockSpec((step, BLK, BLK), lambda i, mine: (i, 0, 0)),
                whole,
            ],
            out_specs=whole,
        ),
        out_shape=jax.ShapeDtypeStruct(start.shape, jnp.float32),
        compiler_params=pltpu.CompilerParams(vmem_limit_bytes=32 << 20),
        cost_estimate=pl.CostEstimate(
            flops=slots * bands * BLK * BLK * 2,
            bytes_accessed=slots * BLK * (bands + BLK) * 2,
            transcendentals=0,
        ),
        name="apply",
    )(mine, values, kernel_tiles, start)


def exchange(values):
    return lax.all_to_all(values, AXES, split_axis=0, concat_axis=0, tiled=True)


def on_device(
    emission, positions, normals, areas, material, reflect, pair_local, pair_device, pair_block
):
    bands, patches = emission.shape
    blocks = patches // BLK
    devices = lax.axis_size(AXES)
    me = lax.axis_index(AXES)
    pairs = pair_local.shape[0]
    areas = areas[None, :]

    target = pair_device[:, 0]
    order = jnp.arange(pairs, dtype=jnp.int32)
    earlier = (target[:, None] == target[None, :]) & (order[None, :] < order[:, None])
    slot = target * 2 + jnp.sum(earlier.astype(jnp.int32), 1)
    code = pair_block * blocks + pair_local
    own = jnp.max(
        jnp.where(
            slot[:, None] == jnp.arange(2 * devices, dtype=jnp.int32)[None, :], code[:, None], -1
        ),
        0,
    )
    everyone = lax.all_gather(own, AXES, axis=0, tiled=False).reshape(devices, devices, 2)
    asked = lax.dynamic_index_in_dim(everyone, me, 1, keepdims=False)
    own = own.reshape(devices, 2)

    geometry = jnp.concatenate([positions, normals], 0).reshape(6, blocks, BLK).transpose(1, 0, 2)
    all_geometry = lax.all_gather(geometry, AXES, axis=0, tiled=True)

    first_block = (jnp.arange(devices, dtype=jnp.int32) * blocks)[:, None]
    send_near = jnp.where(own >= 0, own % blocks, 0).reshape(-1)
    send_far = jnp.where(asked >= 0, asked // blocks, 0).reshape(-1)
    near_mine = jnp.where(asked >= 0, asked // blocks, -1).reshape(-1)
    near_other = (first_block + jnp.where(asked >= 0, asked % blocks, 0)).reshape(-1)
    far_mine = jnp.where(own >= 0, own % blocks, -1).reshape(-1)
    far_other = (first_block + jnp.where(own >= 0, own // blocks, 0)).reshape(-1)

    class_hot = (
        jnp.arange(reflect.shape[1], dtype=jnp.int32)[:, None] == material[None, :]
    ).astype(jnp.float32)
    albedo = jnp.dot(reflect, class_hot, precision=lax.Precision.HIGHEST)

    near_tiles = tiles(near_mine, near_other, geometry, all_geometry)
    far_tiles = tiles(far_mine, far_other, geometry, all_geometry)
    current = emission
    for sweep_index in range(SWEEPS):
        near_values = exchange(pack(send_near, current, areas))
        far_values = exchange(pack(send_far, current, areas))
        gathered = apply(near_mine, near_values, near_tiles, jnp.zeros_like(emission))
        gathered = apply(far_mine, far_values, far_tiles, gathered)
        current = emission + albedo * gathered
    return current


def solution(mesh):
    return jax.shard_map(
        on_device,
        mesh=mesh,
        in_specs=(
            P(None, AXES),
            P(None, AXES),
            P(None, AXES),
            P(AXES),
            P(AXES),
            P(),
            P(AXES),
            P(AXES, None),
            P(AXES),
        ),
        out_specs=P(None, AXES),
        check_vma=False,
    )
```

profile of v0, /device:TPU:1, one launch (start us, length us, event | category | flops | bytes accessed | tf_op | source)
XLA Modules:
  0.0 505.7 jit_solution(6894149039823487758)
XLA Ops:
  10.8 1.2 copy-done.10
  13.8 1.9 copy-done.6
  15.7 12.0 %all-to-all-start.1 = ((bf16[256,64,128]{2,1,0:T(8,128)(2,1)}), bf16[256,64,128]{2,1,0:T(8,128)(2,1)}, u32[]{:S(2)}, u32[]{:S(2)}) async-start(bf16[256,64,128]{2,1,0:T(8,128)(2,1)} %copy-done.6), calls=%async_computation.1 | async-start | bytes 8388608 | tf_op jit(solution)/shard_map/all_to_all | solution.py:152
  27.7 94.0 %all-gather.1 = s32[128,1,256]{2,1,0:T(1,128)S(1)} all-gather(s32[1,1,256]{2,1,0:T(1,128)S(1)} %bitcast.24), channel_id=2, replica_groups=mesh['grp'=8,'dev'=16] {'grp','dev'}, dimensions={0}, use_global_device_ids=true | all-gather | bytes 132096 | tf_op jit(solution)/shard_map/all_gather | solution.py:176
  123.1 2.1 copy-done.7
  125.2 6.7 %all-to-all-start = ((bf16[256,64,128]{2,1,0:T(8,128)(2,1)}), bf16[256,64,128]{2,1,0:T(8,128)(2,1)}, u32[]{:S(2)}, u32[]{:S(2)}) async-start(bf16[256,64,128]{2,1,0:T(8,128)(2,1)} %copy-done.7), calls=%async_computation | async-start | bytes 8388608 | tf_op jit(solution)/shard_map/all_to_all | solution.py:152
  132.0 15.5 %copy.21.geometry_ref = f32[4096,6,128]{2,1,0:T(8,128)} copy(f32[4096,6,128]{2,0,1:T(8,128)} %all-gather.4.cloned.1.call-done) | data formatting | bytes 25165824 | tf_op jit(solution)/shard_map/all_gather | solution.py:181
  147.5 40.4 %tiles.3.tiles_ref = bf16[256,128,128]{2,1,0:T(8,128)(2,1)S(1)} custom-call(s32[256]{0:T(256)S(1)} %get-tuple-element.5.mine_ref, s32[256]{0:T(256)S(1)} %get-tuple-element.7.other_ref, f32[32,6,128]{2,1,0:T(8,128)S(1)} %maximum_bitcast_fusion.own_geometry_ref, f32[4096,6,128]{2,1,0:T(8,128)} %copy.21.geometry_ref), custom_call_target="tpu_custom_call" | custom-call | flops 125829120 | bytes 8388608 | tf_op jit(solution)/shard_map/tiles/pallas_call | solution.py:85
  187.9 47.7 %tiles.2.tiles_ref = bf16[256,128,128]{2,1,0:T(8,128)(2,1)S(1)} custom-call(s32[256]{0:T(256)S(1)} %get-tuple-element.10.mine_ref, s32[256]{0:T(256)S(1)} %get-tuple-element.9.other_ref, f32[32,6,128]{2,1,0:T(8,128)S(1)} %maximum_bitcast_fusion.own_geometry_ref, f32[4096,6,128]{2,1,0:T(8,128)} %copy.21.geometry_ref), custom_call_target="tpu_custom_call" | custom-call | flops 125829120 | bytes 8388608 | tf_op jit(solution)/shard_map/tiles/pallas_call | solution.py:85
  235.7 3.2 copy-done.1
  239.0 23.4 %apply.4.start_ref = f32[64,4096]{1,0:T(8,128)S(1)} custom-call(s32[256]{0:T(256)S(1)} %get-tuple-element.5.mine_ref, bf16[256,64,128]{2,1,0:T(8,128)(2,1)} %all-to-all-done.1.values_ref, bf16[256,128,128]{2,1,0:T(8,128)(2,1)S(1)} %tiles.3.tiles_ref, f32[64,4096]{1,0:T(8,128)S(1)} %broadcast_5_start_ref.2.start_ref), custom_call_target="tpu_custom_call" | custom-call | flops 536870912 | bytes 12582912 | tf_op jit(solution)/shard_map/apply/pallas_call | solution.py:128
  262.4 3.4 copy-done.2
  265.8 24.9 %apply.5 = f32[64,4096]{1,0:T(8,128)S(1)} custom-call(s32[256]{0:T(256)S(1)} %get-tuple-element.10.mine_ref, bf16[256,64,128]{2,1,0:T(8,128)(2,1)} %all-to-all-done.values_ref, bf16[256,128,128]{2,1,0:T(8,128)(2,1)S(1)} %copy-done.2, f32[64,4096]{1,0:T(8,128)S(1)} %apply.4.start_ref), custom_call_target="tpu_custom_call" | custom-call | flops 536870912 | bytes 12582912 | tf_op jit(solution)/shard_map/apply/pallas_call | solution.py:128
  290.7 1.7 multiply_add_fusion.1
  293.4 2.0 copy-done.9
  295.4 64.0 %all-to-all-start.3 = ((bf16[256,64,128]{2,1,0:T(8,128)(2,1)}), bf16[256,64,128]{2,1,0:T(8,128)(2,1)}, u32[]{:S(2)}, u32[]{:S(2)}) async-start(bf16[256,64,128]{2,1,0:T(8,128)(2,1)} %copy-done.9), calls=%async_computation.3 | async-start | bytes 8388608 | tf_op jit(solution)/shard_map/all_to_all | solution.py:152
  360.5 2.0 copy-done.8
  362.5 49.0 %all-to-all-done.3.values_ref = bf16[256,64,128]{2,1,0:T(8,128)(2,1)} async-done(((bf16[256,64,128]{2,1,0:T(8,128)(2,1)}), bf16[256,64,128]{2,1,0:T(8,128)(2,1)}, u32[]{:S(2)}, u32[]{:S(2)}) %all-to-all-start.3) | async-done | bytes 4194336 | tf_op jit(solution)/shard_map/all_to_all | solution.py:152
  411.4 6.0 %all-to-all-start.2 = ((bf16[256,64,128]{2,1,0:T(8,128)(2,1)}), bf16[256,64,128]{2,1,0:T(8,128)(2,1)}, u32[]{:S(2)}, u32[]{:S(2)}) async-start(bf16[256,64,128]{2,1,0:T(8,128)(2,1)} %copy-done.8), calls=%async_computation.2 | async-start | bytes 8388608 | tf_op jit(solution)/shard_map/all_to_all | solution.py:152
  417.4 3.4 copy-done.5
  420.8 23.4 %apply.6.start_ref = f32[64,4096]{1,0:T(8,128)S(1)} custom-call(s32[256]{0:T(256)S(1)} %get-tuple-element.5.mine_ref, bf16[256,64,128]{2,1,0:T(8,128)(2,1)} %all-to-all-done.3.values_ref, bf16[256,128,128]{2,1,0:T(8,128)(2,1)S(1)} %copy-done.5, f32[64,4096]{1,0:T(8,128)S(1)} %broadcast_5_start_ref.2.start_ref), custom_call_target="tpu_custom_call" | custom-call | flops 536870912 | bytes 12582912 | tf_op jit(solution)/shard_map/apply/pallas_call | solution.py:128
  444.2 25.2 %all-to-all-done.2.values_ref = bf16[256,64,128]{2,1,0:T(8,128)(2,1)} async-done(((bf16[256,64,128]{2,1,0:T(8,128)(2,1)}), bf16[256,64,128]{2,1,0:T(8,128)(2,1)}, u32[]{:S(2)}, u32[]{:S(2)}) %all-to-all-start.2) | async-done | bytes 4194336 | tf_op jit(solution)/shard_map/all_to_all | solution.py:152
  469.4 3.4 copy-done.3
  472.8 24.9 %apply.7 = f32[64,4096]{1,0:T(8,128)S(1)} custom-call(s32[256]{0:T(256)S(1)} %get-tuple-element.10.mine_ref, bf16[256,64,128]{2,1,0:T(8,128)(2,1)} %all-to-all-done.2.values_ref, bf16[256,128,128]{2,1,0:T(8,128)(2,1)S(1)} %copy-done.3, f32[64,4096]{1,0:T(8,128)S(1)} %apply.6.start_ref), custom_call_target="tpu_custom_call" | custom-call | flops 536870912 | bytes 12582912 | tf_op jit(solution)/shard_map/apply/pallas_call | solution.py:128
  (50 shorter events, 10.7 us)
Async XLA Ops:
  6.5 284.2 %copy-start = (f32[64,16]{0,1:T(8,128)S(1)}, f32[64,16]{0,1:T(8,128)}, u32[]{:S(2)}) copy-start(f32[64,16]{0,1:T(8,128)} %param.14) | copy-start | bytes 12292
  6.5 125.4 %all-gather.4.cloned.1.call-start = ((), (), s32[]{:S(2)}) async-start(), calls=%async_computation.4 | async-start | bytes 12681216 | tf_op jit(solution)/shard_map/all_gather | solution.py:181
  10.8 1.2 copy-start.10
  12.0 0.7 copy-start.12
  13.8 1.9 copy-start.6
  15.7 106.3 %copy-start.11 = (f32[64,4096]{1,0:T(8,128)S(1)}, f32[64,4096]{1,0:T(8,128)}, u32[]{:S(2)}) copy-start(f32[64,4096]{1,0:T(8,128)} %current_ref.3) | copy-start | bytes 3145732
  15.7 106.4 %copy-start.13 = (f32[4096]{0:T(1024)S(1)}, f32[4096]{0:T(1024)}, u32[]{:S(2)}) copy-start(f32[4096]{0:T(1024)} %param.12) | copy-start | bytes 49156
  15.7 109.5 %all-to-all-start.1 = ((bf16[256,64,128]{2,1,0:T(8,128)(2,1)}), bf16[256,64,128]{2,1,0:T(8,128)(2,1)}, u32[]{:S(2)}, u32[]{:S(2)}) async-start(bf16[256,64,128]{2,1,0:T(8,128)(2,1)} %copy-done.6), calls=%async_computation.1 | async-start | bytes 8388608 | tf_op jit(solution)/shard_map/all_to_all | solution.py:152
  123.1 2.1 copy-start.7
  125.2 137.2 %all-to-all-start = ((bf16[256,64,128]{2,1,0:T(8,128)(2,1)}), bf16[256,64,128]{2,1,0:T(8,128)(2,1)}, u32[]{:S(2)}, u32[]{:S(2)}) async-start(bf16[256,64,128]{2,1,0:T(8,128)(2,1)} %copy-done.7), calls=%async_computation | async-start | bytes 8388608 | tf_op jit(solution)/shard_map/all_to_all | solution.py:152
  187.9 51.0 %copy-start.4 = (bf16[256,128,128]{2,1,0:T(8,128)(2,1)}, bf16[256,128,128]{2,1,0:T(8,128)(2,1)S(1)}, u32[]{:S(2)}) copy-start(bf16[256,128,128]{2,1,0:T(8,128)(2,1)S(1)} %tiles.3.tiles_ref) | copy-start | bytes 25165828
  235.6 3.2 copy-start.1
  262.4 3.4 copy-start.2
  265.8 24.9 %copy-start.15 = (s32[4096]{0:T(1024)S(1)}, s32[4096]{0:T(1024)}, u32[]{:S(2)}) copy-start(s32[4096]{0:T(1024)} %param.13) | copy-start | bytes 49156
  293.4 2.0 copy-start.9
  295.4 116.0 %all-to-all-start.3 = ((bf16[256,64,128]{2,1,0:T(8,128)(2,1)}), bf16[256,64,128]{2,1,0:T(8,128)(2,1)}, u32[]{:S(2)}, u32[]{:S(2)}) async-start(bf16[256,64,128]{2,1,0:T(8,128)(2,1)} %copy-done.9), calls=%async_computation.3 | async-start | bytes 8388608 | tf_op jit(solution)/shard_map/all_to_all | solution.py:152
  360.5 2.0 copy-start.8
  411.4 58.0 %all-to-all-start.2 = ((bf16[256,64,128]{2,1,0:T(8,128)(2,1)}), bf16[256,64,128]{2,1,0:T(8,128)(2,1)}, u32[]{:S(2)}, u32[]{:S(2)}) async-start(bf16[256,64,128]{2,1,0:T(8,128)(2,1)} %copy-done.8), calls=%async_computation.2 | async-start | bytes 8388608 | tf_op jit(solution)/shard_map/all_to_all | solution.py:152
  417.4 3.4 copy-start.5
  469.4 3.4 copy-start.3
  472.8 24.9 %copy-start.14 = (f32[64,4096]{1,0:T(8,128)S(1)}, f32[64,4096]{1,0:T(8,128)}, u32[]{:S(2)}) copy-start(f32[64,4096]{1,0:T(8,128)} %get-tuple-element.12) | copy-start | bytes 3145732
Sparse Core Ops, SparseCore 0:
  10.4 119.5 all-gather.3
where the time goes:
time: 509 us; the launch traced here: 506 us
  Pallas kernels  189 us (37%)
  blocking collectives  94 us (18%)
  starting transfers between devices  88.7 us (17%)
  waiting for transfers between devices  74.2 us (15%)
  local copies, waits for them, and re-layouts  40.2 us (8%)
  between operations  13.7 us (3%)
    pallas_call x4, Pallas kernels, apply(): pl.pallas_call(apply_kernel, grid_spec=pltpu.PrefetchScalarGridSpec(num_s...  96.6 us
    all_gather x1, blocking collectives, on_device(): lax.all_gather(own, AXES, axis=0, tiled=False).reshape(devices, devices, 2)  94 us
    all_to_all x4, starting transfers between devices, exchange(): return lax.all_to_all(values, AXES, split_axis=0, concat_axis=0, tiled=True)  88.7 us
    pallas_call x2, Pallas kernels, tiles(): pl.pallas_call(tiles_kernel, grid_spec=pltpu.PrefetchScalarGridSpec(num_s...  88.1 us
    all_to_all x4, waiting for transfers between devices, exchange(): return lax.all_to_all(values, AXES, split_axis=0, concat_axis=0, tiled=True)  74.2 us
    unnamed x32, local copies, waits for them, and re-layouts  23.3 us
    all_gather x1, local copies, waits for them, and re-layouts, on_device(): all_geometry = lax.all_gather(geometry, AXES, axis=0, tiled=True)  15.5 us
  transfers between devices with their start and end apart: 5, of which 2 were waited for; matrix products, arithmetic and copies ran while one was open for 4% of the time, Pallas kernels for 27%

commit v1 on v0

--- a/solution.py
+++ b/solution.py
@@ -148,8 +148,83 @@
     )(mine, values, kernel_tiles, start)
 
 
+def torus_order():
+    seen = set()
+    groups = []
+    for dx in range(4):
+        for dy in range(4):
+            for dz in range(4):
+                for core in range(2):
+                    group = []
+                    for x, y, z in ((dx, dy, dz), (dy, dz, dx), (dz, dx, dy)):
+                        for step in ((x, core, y, z), (-x % 4, core, -y % 4, -z % 4)):
+                            if step not in seen and any(step):
+                                seen.add(step)
+                                group.append(step)
+                    if group:
+                        groups.append(group)
+    groups.sort(key=lambda group: sum(min(v, 4 - v) for v in group[0][:1] + group[0][2:]))
+    return [step for group in groups for step in group]
+
+
+ORDER = torus_order()
+
+
+def peer(grp, dev, step):
+    x, core, y, z = step
+    return (
+        lax.rem(grp // 2 + x, 4) * 2 + lax.rem(lax.rem(grp, 2) + core, 2),
+        lax.rem(dev // 4 + y, 4) * 4 + lax.rem(lax.rem(dev, 4) + z, 4),
+    )
+
+
+def exchange_kernel(send_ref, out_ref, send_sem, recv_sem, local_sem):
+    grp, dev = lax.axis_index("grp"), lax.axis_index("dev")
+    me = grp * 16 + dev
+    slots = send_ref.shape[0] // 128
+    barrier = pltpu.get_barrier_semaphore()
+    for step in ORDER:
+        pl.semaphore_signal(
+            barrier, inc=1, device_id=peer(grp, dev, step), device_id_type=pl.DeviceIdType.MESH
+        )
+    pl.semaphore_wait(barrier, len(ORDER))
+    copies = []
+    for place, step in enumerate(ORDER):
+        other = peer(grp, dev, step)
+        copies.append(
+            pltpu.make_async_remote_copy(
+                src_ref=send_ref.at[pl.ds((other[0] * 16 + other[1]) * slots, slots)],
+                dst_ref=out_ref.at[pl.ds(me * slots, slots)],
+                send_sem=send_sem.at[place],
+                recv_sem=recv_sem.at[place],
+                device_id=other,
+                device_id_type=pl.DeviceIdType.MESH,
+            )
+        )
+        copies[-1].start()
+    local = pltpu.make_async_copy(
+        send_ref.at[pl.ds(me * slots, slots)], out_ref.at[pl.ds(me * slots, slots)], local_sem
+    )
+    local.start()
+    local.wait()
+    for copy in copies:
+        copy.wait()
+
+
 def exchange(values):
-    return lax.all_to_all(values, AXES, split_axis=0, concat_axis=0, tiled=True)
+    return pl.pallas_call(
+        exchange_kernel,
+        in_specs=[pl.BlockSpec(memory_space=pl.ANY)],
+        out_specs=pl.BlockSpec(memory_space=pl.ANY),
+        out_shape=jax.ShapeDtypeStruct(values.shape, values.dtype),
+        scratch_shapes=[
+            pltpu.SemaphoreType.DMA((len(ORDER),)),
+            pltpu.SemaphoreType.DMA((len(ORDER),)),
+            pltpu.SemaphoreType.DMA,
+        ],
+        compiler_params=pltpu.CompilerParams(collective_id=0, has_side_effects=True),
+        name="exchange",
+    )(values)
 
 
 def on_device(

time: 509 us -> 603 us (1.18)
  Pallas kernels: 189 us -> 480 us
  starting transfers between devices: 88.7 us -> 0.01 us
  waiting for transfers between devices: 74.2 us -> 0.04 us
  blocking collectives: 94 us -> 54.3 us
  local copies, waits for them, and re-layouts: 40.2 us -> 47.3 us
    pallas_call x0 -> x4, Pallas kernels: none -> 324 us  [exchange(): pl.pallas_call(exchange_kernel, in_specs=[pl.BlockSpec(memory_space=pl.AN...]
    all_to_all x4 -> x0, starting transfers between devices: 88.7 us -> none  [exchange(): return lax.all_to_all(values, AXES, split_axis=0, concat_axis=0, tiled=True)]
    all_to_all x4 -> x0, waiting for transfers between devices: 74.2 us -> none  [exchange(): return lax.all_to_all(values, AXES, split_axis=0, concat_axis=0, tiled=True)]
    all_gather x1, blocking collectives: 94 us -> 54.3 us  [on_device(): lax.all_gather(own, AXES, axis=0, tiled=False).reshape(devices, devices, 2)]
    pallas_call x4, Pallas kernels: 96.6 us -> 66.6 us  [apply(): pl.pallas_call(apply_kernel, grid_spec=pltpu.PrefetchScalarGridSpec(num_s...]
    unnamed x32 -> x40, local copies, waits for them, and re-layouts: 23.3 us -> 30.4 us
  transfers between devices with their start and end apart: 5 -> 1, of which waited for: 2 -> 0; matrix products, arithmetic and copies ran while one was open for 4% -> 0% of each run, Pallas kernels for 27% -> 21%
where the time goes in v1:
time: 603 us; the launch traced here: 602 us
  Pallas kernels  480 us (80%)
  blocking collectives  54.3 us (9%)
  local copies, waits for them, and re-layouts  47.3 us (8%)
  between operations  13.7 us (2%)
    pallas_call x4, Pallas kernels, exchange(): pl.pallas_call(exchange_kernel, in_specs=[pl.BlockSpec(memory_space=pl.AN...  324 us
    pallas_call x2, Pallas kernels, tiles(): pl.pallas_call(tiles_kernel, grid_spec=pltpu.PrefetchScalarGridSpec(num_s...  86 us
    pallas_call x4, Pallas kernels, apply(): pl.pallas_call(apply_kernel, grid_spec=pltpu.PrefetchScalarGridSpec(num_s...  66.6 us
    all_gather x1, blocking collectives, on_device(): lax.all_gather(own, AXES, axis=0, tiled=False).reshape(devices, devices, 2)  54.3 us
    unnamed x40, local copies, waits for them, and re-layouts  30.4 us
    all_gather x1, local copies, waits for them, and re-layouts, on_device(): all_geometry = lax.all_gather(geometry, AXES, axis=0, tiled=True)  15.5 us
  transfers between devices with their start and end apart: 1, of which 0 were waited for; matrix products, arithmetic and copies ran while one was open for 0% of the time, Pallas kernels for 21%

profile of v1, /device:TPU:1, one launch (start us, length us, event | category | flops | bytes accessed | tf_op | source)
XLA Modules:
  0.0 602.0 jit_solution(8426435184325117258)
XLA Ops:
  10.5 54.3 %all-gather.1 = s32[128,1,256]{2,1,0:T(1,128)S(1)} all-gather(s32[1,1,256]{2,1,0:T(1,128)S(1)} %bitcast.24), channel_id=2, replica_groups=mesh['grp'=8,'dev'=16] {'grp','dev'}, dimensions={0}, use_global_device_ids=true | all-gather | bytes 132096 | tf_op jit(solution)/shard_map/all_gather | solution.py:251
  65.5 1.2 copy-done.14
  68.5 1.9 copy-done.8
  70.4 68.1 %exchange.5.values_ref = bf16[256,64,128]{2,1,0:T(8,128)(2,1)} custom-call(bf16[256,64,128]{2,1,0:T(8,128)(2,1)} %copy-done.8), custom_call_target="tpu_custom_call" | custom-call | tf_op jit(solution)/shard_map/exchange/pallas_call | solution.py:215
  139.7 1.9 copy-done.9
  141.6 58.7 %exchange.4.values_ref = bf16[256,64,128]{2,1,0:T(8,128)(2,1)} custom-call(bf16[256,64,128]{2,1,0:T(8,128)(2,1)} %copy-done.9), custom_call_target="tpu_custom_call" | custom-call | tf_op jit(solution)/shard_map/exchange/pallas_call | solution.py:215
  200.4 15.5 %copy.21.geometry_ref = f32[4096,6,128]{2,1,0:T(8,128)} copy(f32[4096,6,128]{2,0,1:T(8,128)} %all-gather.4.cloned.1.call-done) | data formatting | bytes 25165824 | tf_op jit(solution)/shard_map/all_gather | solution.py:256
  215.9 40.4 %tiles.3.tiles_ref = bf16[256,128,128]{2,1,0:T(8,128)(2,1)S(1)} custom-call(s32[256]{0:T(256)S(1)} %get-tuple-element.5.mine_ref, s32[256]{0:T(256)S(1)} %get-tuple-element.7.other_ref, f32[32,6,128]{2,1,0:T(8,128)S(1)} %maximum_bitcast_fusion.own_geometry_ref, f32[4096,6,128]{2,1,0:T(8,128)} %copy.21.geometry_ref), custom_call_target="tpu_custom_call" | custom-call | flops 125829120 | bytes 8388608 | tf_op jit(solution)/shard_map/tiles/pallas_call | solution.py:85
  256.4 3.2 copy-done.3
  259.6 45.6 %tiles.2.tiles_ref = bf16[256,128,128]{2,1,0:T(8,128)(2,1)S(1)} custom-call(s32[256]{0:T(256)S(1)} %get-tuple-element.10.mine_ref, s32[256]{0:T(256)S(1)} %get-tuple-element.9.other_ref, f32[32,6,128]{2,1,0:T(8,128)S(1)} %maximum_bitcast_fusion.own_geometry_ref, f32[4096,6,128]{2,1,0:T(8,128)} %copy.21.geometry_ref), custom_call_target="tpu_custom_call" | custom-call | flops 125829120 | bytes 8388608 | tf_op jit(solution)/shard_map/tiles/pallas_call | solution.py:85
  305.3 6.3 %copy-done.4 = bf16[256,128,128]{2,1,0:T(8,128)(2,1)S(1)} copy-done((bf16[256,128,128]{2,1,0:T(8,128)(2,1)S(1)}, bf16[256,128,128]{2,1,0:T(8,128)(2,1)}, u32[]{:S(2)}) %copy-start.4) | copy-done | bytes 8388632
  311.6 15.5 %apply.4.start_ref = f32[64,4096]{1,0:T(8,128)S(1)} custom-call(s32[256]{0:T(256)S(1)} %get-tuple-element.5.mine_ref, bf16[256,64,128]{2,1,0:T(8,128)(2,1)S(1)} %copy-done.10, bf16[256,128,128]{2,1,0:T(8,128)(2,1)S(1)} %copy-done.4, f32[64,4096]{1,0:T(8,128)S(1)} %broadcast_5_start_ref.2.start_ref), custom_call_target="tpu_custom_call" | custom-call | flops 536870912 | bytes 12582912 | tf_op jit(solution)/shard_map/apply/pallas_call | solution.py:128
  327.1 17.9 %apply.5 = f32[64,4096]{1,0:T(8,128)S(1)} custom-call(s32[256]{0:T(256)S(1)} %get-tuple-element.10.mine_ref, bf16[256,64,128]{2,1,0:T(8,128)(2,1)S(1)} %copy-done.11, bf16[256,128,128]{2,1,0:T(8,128)(2,1)S(1)} %tiles.2.tiles_ref, f32[64,4096]{1,0:T(8,128)S(1)} %apply.4.start_ref), custom_call_target="tpu_custom_call" | custom-call | flops 536870912 | bytes 12582912 | tf_op jit(solution)/shard_map/apply/pallas_call | solution.py:128
  345.0 1.7 multiply_add_fusion.1
  347.8 1.9 copy-done.7
  350.7 2.0 copy-done.6
  352.7 119.2 %exchange.7.values_ref = bf16[256,64,128]{2,1,0:T(8,128)(2,1)} custom-call(bf16[256,64,128]{2,1,0:T(8,128)(2,1)} %copy-done.7), custom_call_target="tpu_custom_call" | custom-call | tf_op jit(solution)/shard_map/exchange/pallas_call | solution.py:215
  471.9 3.4 copy-done.5
  475.3 2.2 copy-done.12
  477.5 15.5 %apply.6.start_ref = f32[64,4096]{1,0:T(8,128)S(1)} custom-call(s32[256]{0:T(256)S(1)} %get-tuple-element.5.mine_ref, bf16[256,64,128]{2,1,0:T(8,128)(2,1)S(1)} %copy-done.12, bf16[256,128,128]{2,1,0:T(8,128)(2,1)S(1)} %copy-done.5, f32[64,4096]{1,0:T(8,128)S(1)} %broadcast_5_start_ref.2.start_ref), custom_call_target="tpu_custom_call" | custom-call | flops 536870912 | bytes 12582912 | tf_op jit(solution)/shard_map/apply/pallas_call | solution.py:128
  492.9 77.7 %exchange.6.values_ref = bf16[256,64,128]{2,1,0:T(8,128)(2,1)} custom-call(bf16[256,64,128]{2,1,0:T(8,128)(2,1)} %copy-done.6), custom_call_target="tpu_custom_call" | custom-call | tf_op jit(solution)/shard_map/exchange/pallas_call | solution.py:215
  570.6 3.4 copy-done.2
  574.0 2.2 copy-done.13
  576.2 17.8 %apply.7 = f32[64,4096]{1,0:T(8,128)S(1)} custom-call(s32[256]{0:T(256)S(1)} %get-tuple-element.10.mine_ref, bf16[256,64,128]{2,1,0:T(8,128)(2,1)S(1)} %copy-done.13, bf16[256,128,128]{2,1,0:T(8,128)(2,1)S(1)} %copy-done.2, f32[64,4096]{1,0:T(8,128)S(1)} %apply.6.start_ref), custom_call_target="tpu_custom_call" | custom-call | flops 536870912 | bytes 12582912 | tf_op jit(solution)/shard_map/apply/pallas_call | solution.py:128
  (54 shorter events, 10.8 us)
Async XLA Ops:
  6.5 338.4 %copy-start = (f32[64,16]{0,1:T(8,128)S(1)}, f32[64,16]{0,1:T(8,128)}, u32[]{:S(2)}) copy-start(f32[64,16]{0,1:T(8,128)} %param.14) | copy-start | bytes 12292
  6.5 193.8 %all-gather.4.cloned.1.call-start = ((), (), s32[]{:S(2)}) async-start(), calls=%async_computation | async-start | bytes 12681216 | tf_op jit(solution)/shard_map/all_gather | solution.py:256
  65.5 1.2 copy-start.14
  66.7 0.7 copy-start.16
  68.5 1.9 copy-start.8
  70.4 68.1 %copy-start.15 = (f32[64,4096]{1,0:T(8,128)S(1)}, f32[64,4096]{1,0:T(8,128)}, u32[]{:S(2)}) copy-start(f32[64,4096]{1,0:T(8,128)} %current_ref.3) | copy-start | bytes 3145732
  70.4 68.1 %copy-start.17 = (f32[4096]{0:T(1024)S(1)}, f32[4096]{0:T(1024)}, u32[]{:S(2)}) copy-start(f32[4096]{0:T(1024)} %param.12) | copy-start | bytes 49156
  139.6 1.9 copy-start.9
  256.4 3.2 copy-start.3
  259.6 45.7 %copy-start.10 = (bf16[256,64,128]{2,1,0:T(8,128)(2,1)S(1)}, bf16[256,64,128]{2,1,0:T(8,128)(2,1)}, u32[]{:S(2)}) copy-start(bf16[256,64,128]{2,1,0:T(8,128)(2,1)} %exchange.5.values_ref) | copy-start | bytes 12582916
  305.2 21.9 %copy-start.1 = (bf16[256,128,128]{2,1,0:T(8,128)(2,1)}, bf16[256,128,128]{2,1,0:T(8,128)(2,1)S(1)}, u32[]{:S(2)}) copy-start(bf16[256,128,128]{2,1,0:T(8,128)(2,1)S(1)} %tiles.2.tiles_ref) | copy-start | bytes 25165828
  305.3 6.3 %copy-start.4 = (bf16[256,128,128]{2,1,0:T(8,128)(2,1)S(1)}, bf16[256,128,128]{2,1,0:T(8,128)(2,1)}, u32[]{:S(2)}) copy-start(bf16[256,128,128]{2,1,0:T(8,128)(2,1)} %copy-done.3) | copy-start | bytes 25165828
  311.6 15.5 %copy-start.11 = (bf16[256,64,128]{2,1,0:T(8,128)(2,1)S(1)}, bf16[256,64,128]{2,1,0:T(8,128)(2,1)}, u32[]{:S(2)}) copy-start(bf16[256,64,128]{2,1,0:T(8,128)(2,1)} %exchange.4.values_ref) | copy-start | bytes 12582916
  327.1 17.9 %copy-start.19 = (s32[4096]{0:T(1024)S(1)}, s32[4096]{0:T(1024)}, u32[]{:S(2)}) copy-start(s32[4096]{0:T(1024)} %param.13) | copy-start | bytes 49156
  347.7 1.9 copy-start.7
  350.7 2.0 copy-start.6
  471.9 3.4 copy-start.5
  475.3 2.2 copy-start.12
  570.6 3.4 copy-start.2
  574.0 2.2 copy-start.13
  576.2 17.8 %copy-start.18 = (f32[64,4096]{1,0:T(8,128)S(1)}, f32[64,4096]{1,0:T(8,128)}, u32[]{:S(2)}) copy-start(f32[64,4096]{1,0:T(8,128)} %get-tuple-element.12) | copy-start | bytes 3145732
Sparse Core Ops, SparseCore 0:
  10.4 99.5 all-gather.3
